TPU v7x, 32 devices: a whole 2x2x4 slice. The times are simulated.
32 devices in a mesh: dp: 8 (over z, x), expert: 4 (over y, core).
Axes of the slice: x: 2, y: 2, z: 4, core: 2. Of those that a mesh axis runs over, the one named last changes fastest.
Arguments:
- tokens: bfloat16 [16384, 1024], P(('dp', 'expert')), may hold values from -6 to 6
- block_expert: int32 [128], P(('dp', 'expert')), may hold values from 0 to 31, as said below
- gate_weight: bfloat16 [32, 1024, 384], P('expert'), may hold values from -0.1875 to 0.1875
- up_weight: bfloat16 [32, 1024, 384], P('expert'), may hold values from -0.1875 to 0.1875
Outputs:
- gram_factor: float32 [32, 384, 384], P('expert', 'dp')
Inputs may be any that keep to these rules, and one draw needn't show every extreme that they name: `block_expert`: expert e is held by index e // 8 of the expert axis. Among the 4 blocks of one device, at most 1 name experts of any one index of the expert axis; in every group of devices along the expert axis, one index of the expert axis receives exactly 1 block from every device of the group.
All inputs are finite; a program needn't handle non-finite values.
Results may differ from a plain program's by a relative error of at most 0.0031.
Values may be sent and summed in bfloat16 or wider, within the bound.
A program may use at most 128 MiB of HBM per device.

v0:
```python
import jax
import jax.numpy as jnp
from jax import lax
from jax.sharding import PartitionSpec as P

BLOCK = 128


RIDGE = 0.05


def slot_ranks(assigned, experts_each, owners):
    owner_of = assigned // experts_each
    columns = jnp.arange(owners, dtype=jnp.int32)
    marked = (owner_of[..., None] == columns).astype(jnp.int32)
    earlier = jnp.cumsum(marked, axis=-2) - marked
    position = jnp.sum(earlier * marked, axis=-1)
    return (owner_of, position)


def upper_factor(matrix):
    lower_part = jnp.linalg.cholesky(matrix)
    return jnp.swapaxes(lower_part, -1, -2)


def on_device(tokens, block_expert, gate_weight, up_weight):
    owners = lax.axis_size("expert")
    member = lax.axis_index("expert")
    replicas = lax.axis_size("dp")
    tok_dev = tokens.shape[0]
    model_width = tokens.shape[1]
    experts_each = gate_weight.shape[0]
    hidden_width = gate_weight.shape[2]
    blocks_dev = tok_dev // BLOCK
    capacity = blocks_dev // 4
    slot_count = owners * capacity
    owner_of, position = slot_ranks(block_expert, experts_each, owners)
    target = owner_of * capacity + position
    select = (target[None, :] == jnp.arange(slot_count, dtype=jnp.int32)[:, None]).astype(
        jnp.bfloat16
    )
    blocked = tokens.reshape(blocks_dev, BLOCK, model_width)
    outgoing = jnp.einsum(
        "sb,bnd->snd", select, blocked, preferred_element_type=jnp.float32
    ).astype(jnp.bfloat16)
    outgoing = outgoing.reshape(owners, capacity, BLOCK, model_width)
    arrived = lax.all_to_all(outgoing, "expert", split_axis=0, concat_axis=0, tiled=True)
    group_assign = lax.all_gather(block_expert, "expert", axis=0, tiled=True).reshape(
        owners, blocks_dev
    )
    source_owner, source_position = slot_ranks(group_assign, experts_each, owners)
    for_member = source_owner == member
    matched = for_member[:, :, None] & (
        source_position[:, :, None] == jnp.arange(capacity, dtype=jnp.int32)[None, None, :]
    )
    local_id = group_assign % experts_each
    expert_hot = (local_id[:, :, None] == jnp.arange(experts_each, dtype=jnp.int32)).astype(
        jnp.float32
    )
    slot_table = jnp.einsum(
        "sbc,sbj->scj", matched.astype(jnp.float32), expert_hot, precision=lax.Precision.HIGHEST
    )
    slot_expert = jnp.sum(matched.astype(jnp.int32) * local_id[:, :, None], axis=1)

    def one_source(gram_acc, entry):
        rows_in, ids, table = entry
        gate_rows = jnp.take(gate_weight, ids, axis=0)
        up_rows = jnp.take(up_weight, ids, axis=0)
        gate_proj = jnp.einsum(
            "snd,sdf->snf", rows_in, gate_rows, preferred_element_type=jnp.float32
        )
        up_proj = jnp.einsum("snd,sdf->snf", rows_in, up_rows, preferred_element_type=jnp.float32)
        hidden = (jax.nn.silu(gate_proj) * up_proj).astype(jnp.bfloat16)
        partial_gram = jnp.einsum(
            "snf,sng->sfg", hidden, hidden, preferred_element_type=jnp.float32
        )
        gram_acc = gram_acc + jnp.einsum(
            "sj,sfg->jfg", table, partial_gram, precision=lax.Precision.HIGHEST
        )
        return (gram_acc, None)

    start_gram = jnp.zeros((experts_each, hidden_width, hidden_width), jnp.float32)
    gram_total, unused = lax.scan(one_source, start_gram, (arrived, slot_expert, slot_table))
    mean_rows = tok_dev * replicas // experts_each
    local_gram = gram_total * (1.0 / mean_rows)
    identity = jnp.eye(hidden_width, dtype=jnp.float32)
    row_count = hidden_width // replicas
    copies = max(1, replicas // experts_each)
    per_device = max(1, experts_each // replicas)
    repeated = jnp.repeat(local_gram, copies, axis=0)
    owned = lax.psum_scatter(repeated, "dp", scatter_dimension=0, tiled=True)
    owned_factor = upper_factor(owned + RIDGE * identity)
    col_count = hidden_width // copies
    copy_index = lax.axis_index("dp") % copies
    column_part = lax.dynamic_slice_in_dim(owned_factor, copy_index * col_count, col_count, 2)
    pieces = column_part.reshape(per_device, replicas, row_count, col_count)
    returned = lax.all_to_all(pieces, "dp", split_axis=1, concat_axis=0, tiled=True)
    returned = returned.reshape(experts_each, copies, row_count, col_count)
    return jnp.swapaxes(returned, 1, 2).reshape(experts_each, row_count, hidden_width)


def solution(mesh):
    placed = (
        P(("dp", "expert"), None),
        P(("dp", "expert")),
        P("expert", None, None),
        P("expert", None, None),
    )
    return jax.shard_map(
        on_device, mesh=mesh, in_specs=placed, out_specs=P("expert", "dp", None), check_vma=False
    )
```

profile of v0, /device:TPU:0, one launch (start us, length us, event | category | flops | bytes accessed | tf_op | source)
XLA Modules:
  0.0 270.9 jit_solution(70803183986653473)
XLA Ops:
  6.5 0.0 copy-start
  6.5 0.0 copy-start.2
  6.5 0.0 copy-start.1
  6.5 0.8 and_select_fusion
  7.3 0.1 fusion.54
  7.4 0.2 select_reduce_fusion.4
  7.6 0.7 fusion.61
  8.3 0.0 copy-done
  8.3 0.9 fusion.38
  9.2 1.3 copy.23
  10.5 4.2 %all-to-all-start = ((bf16[4,1,128,1024]{3,2,1,0:T(8,128)(2,1)}), bf16[4,1,128,1024]{3,2,1,0:T(8,128)(2,1)S(1)}, u32[]{:S(2)}, u32[]{:S(2)}) async-start(bf16[4,1,128,1024]{3,2,1,0:T(8,128)(2,1)} %copy.23), calls=%async_computation | async-start | bytes 2097152 | tf_op jit(solution)/shard_map/all_to_all | solution.py:47
  14.7 0.0 reduce-scatter.2.cloned.1.call-start
  14.7 0.0 copy-done.2
  14.7 0.6 dynamic-slice.6
  16.0 0.0 copy-done.1
  16.0 0.2 dynamic-update-slice.16
  16.2 13.1 %all-reduce.1 = s32[16]{0:T(128)S(1)} all-reduce(s32[16]{0:T(128)S(1)} %dynamic-update-slice.16), channel_id=1, replica_groups=mesh['dp'=8,'expert'=4] {'expert'}, use_global_device_ids=true, to_apply=%add.1 | all-reduce | flops 16 | bytes 128
  29.3 0.1 reshape.322
  29.4 0.1 fusion.47
  29.5 0.1 reshape.325
  29.6 0.2 select_reduce_fusion.3
  29.8 0.1 fusion.53
  30.0 0.2 fusion.48
  30.1 0.0 all-to-all-done
  30.1 42.1 %while.12 = (s32[]{:T(128)}, f32[8,384,384]{2,1,0:T(8,128)}, f32[4,1,8]{2,1,0:T(1,128)S(1)}, bf16[4,1,128,1024]{3,2,1,0:T(8,128)(2,1)S(1)}, s32[4,1]{0,1:T(1,128...) while((s32[]{:T(128)}, f32[8,384,384]{2,1,0:T(8,128)}, ...), condition=%wide.region_6.8_spmd.clone, body=%wide.region_5.7_spmd.clone.sunk | while | flops 243695616 | bytes 13109558 | solution.py:83
  30.1 0.7 constant_dynamic-slice_fusion.3
  32.7 1.4 fusion.73
  34.2 2.0 fusion.74
  36.2 2.7 %select_add_fusion.3 = f32[8,384,384]{2,1,0:T(8,128)} fusion(f32[8,384,384]{2,1,0:T(8,128)} %get-tuple-element.182, f32[384,384]{1,0:T(8,128)S(1)} %fusion.74, f32[8]{0:T(128)S(1)} %fusion.75, pred[]{:T(512)S(6)} %compare.86), kind=kLoop, calls=%fused_computation.clone.1 | loop fusion | flops 3538944 | bytes 10027041 | tf_op jit(solution)/shard_map/while/body/eval_jaxpr/add | solution.py:77
  38.9 0.6 constant_dynamic-slice_fusion.3
  41.5 1.4 fusion.73
  42.9 2.1 fusion.74
  45.0 5.0 %select_add_fusion.3 = f32[8,384,384]{2,1,0:T(8,128)} fusion(f32[8,384,384]{2,1,0:T(8,128)} %get-tuple-element.182, f32[384,384]{1,0:T(8,128)S(1)} %fusion.74, f32[8]{0:T(128)S(1)} %fusion.75, pred[]{:T(512)S(6)} %compare.86), kind=kLoop, calls=%fused_computation.clone.1 | loop fusion | flops 3538944 | bytes 10027041 | tf_op jit(solution)/shard_map/while/body/eval_jaxpr/add | solution.py:77
  50.1 0.6 constant_dynamic-slice_fusion.3
  52.6 1.4 fusion.73
  54.1 2.0 fusion.74
  56.1 5.0 %select_add_fusion.3 = f32[8,384,384]{2,1,0:T(8,128)} fusion(f32[8,384,384]{2,1,0:T(8,128)} %get-tuple-element.182, f32[384,384]{1,0:T(8,128)S(1)} %fusion.74, f32[8]{0:T(128)S(1)} %fusion.75, pred[]{:T(512)S(6)} %compare.86), kind=kLoop, calls=%fused_computation.clone.1 | loop fusion | flops 3538944 | bytes 10027041 | tf_op jit(solution)/shard_map/while/body/eval_jaxpr/add | solution.py:77
  61.2 0.6 constant_dynamic-slice_fusion.3
  63.7 1.4 fusion.73
  65.2 2.0 fusion.74
  67.2 5.0 %select_add_fusion.3 = f32[8,384,384]{2,1,0:T(8,128)} fusion(f32[8,384,384]{2,1,0:T(8,128)} %get-tuple-element.182, f32[384,384]{1,0:T(8,128)S(1)} %fusion.74, f32[8]{0:T(128)S(1)} %fusion.75, pred[]{:T(512)S(6)} %compare.86), kind=kLoop, calls=%fused_computation.clone.1 | loop fusion | flops 3538944 | bytes 10027041 | tf_op jit(solution)/shard_map/while/body/eval_jaxpr/add | solution.py:77
  72.3 6.1 %copy.25 = f32[8,384,384]{1,2,0:T(8,128)} copy(f32[8,384,384]{2,1,0:T(8,128)} %get-tuple-element.43) | data formatting | bytes 9437184 | tf_op jit(solution)/shard_map/while | solution.py:83
  78.3 4.8 %broadcast_multiply_fusion = f32[8,384,384]{1,2,0:T(8,128)} fusion(f32[8,384,384]{1,2,0:T(8,128)} %copy.25), kind=kLoop, calls=%fused_computation.33 | loop fusion | flops 1179648 | bytes 9437184 | tf_op jit(solution)/shard_map/mul | solution.py:85
  83.2 0.0 reduce-scatter.2.cloned.1.call-update
  83.2 96.5 %reduce-scatter.2.cloned.1.call-done = f32[1,384,384]{1,2,0:T(8,128)} async-done(((f32[8,384,384]{1,2,0:T(8,128)}), f32[1,384,384]{1,2,0:T(8,128)}) %reduce-scatter.2.cloned.1.call-update) | async-done | bytes 589840 | tf_op jit(solution)/shard_map/reduce_scatter | solution.py:91
  179.7 1.1 select_add_fusion.1
  180.8 0.2 copy.26
  181.1 1.1 fusion.43
  182.2 11.7 %custom-call.22 = f32[1,128,128]{2,1,0:T(8,128)S(1)} custom-call(f32[1,128,128]{2,1,0:T(8,128)S(1)} %cholesky.189), custom_call_target="Cholesky" | custom-call | tf_op jit(solution)/shard_map/jit(cholesky)/cholesky | solution.py:22
  193.9 0.1 copy.27
  194.1 9.8 %custom-call.23 = f32[1,1,128,128]{2,3,1,0:T(8,128)S(1)} custom-call(f32[1,1,128,128]{3,2,1,0:T(8,128)S(1)} %get-tuple-element.119), custom_call_target="InvertDiagBlocksLowerTriangular" | custom-call | tf_op jit(solution)/shard_map/jit(cholesky)/cholesky | solution.py:22
  203.9 0.3 constant_dynamic-update-slice_fusion.1
  204.3 0.4 fusion.39
  204.7 11.7 %custom-call.24 = f32[1,128,128]{2,1,0:T(8,128)S(1)} custom-call(f32[1,128,128]{2,1,0:T(8,128)S(1)} %cholesky.193), custom_call_target="Cholesky" | custom-call | tf_op jit(solution)/shard_map/jit(cholesky)/cholesky | solution.py:22
  216.4 0.1 copy.28
  216.5 10.0 %custom-call.25 = f32[1,1,128,128]{2,3,1,0:T(8,128)S(1)} custom-call(f32[1,1,128,128]{3,2,1,0:T(8,128)S(1)} %get-tuple-element.117), custom_call_target="InvertDiagBlocksLowerTriangular" | custom-call | tf_op jit(solution)/shard_map/jit(cholesky)/cholesky | solution.py:22
  226.5 0.3 fusion.40
  226.8 0.4 fusion.41
  227.2 11.7 %custom-call.26 = f32[1,128,128]{2,1,0:T(8,128)S(1)} custom-call(f32[1,128,128]{2,1,0:T(8,128)S(1)} %fusion.41), custom_call_target="Cholesky" | custom-call | tf_op jit(solution)/shard_map/jit(cholesky)/cholesky | solution.py:22
  239.0 0.1 copy.29
  239.1 0.7 compare_reduce_fusion
  239.8 0.6 compare_reduce_fusion.1
  242.4 20.9 %all_to_all.14 = f32[1,8,48,384]{3,2,0,1:T(8,128)S(1)} all-to-all(f32[1,8,48,384]{3,2,0,1:T(8,128)S(1)} %bitcast.107), channel_id=1, replica_groups=mesh['dp'=8,'expert'=4] {'dp'}, dimensions={1} | all-to-all | bytes 1179648 | tf_op jit(solution)/shard_map/all_to_all | solution.py:97
  263.3 0.8 copy.49
  (19 shorter events, 0.4 us)
Async XLA Ops:
  6.5 1.7 copy-start
  6.5 8.2 %copy-start.2 = (u32[32]{0:T(128)S(1)}, u32[32]{0:T(128)}, u32[]{:S(2)}) copy-start(u32[32]{0:T(128)} %constant.242) | copy-start | bytes 388
  6.5 9.4 %copy-start.1 = (s32[4]{0:T(128)S(1)}, s32[4]{0:T(128)}, u32[]{:S(2)}) copy-start(s32[4]{0:T(128)} %param.9) | copy-start | bytes 52
  10.5 19.6 %all-to-all-start = ((bf16[4,1,128,1024]{3,2,1,0:T(8,128)(2,1)}), bf16[4,1,128,1024]{3,2,1,0:T(8,128)(2,1)S(1)}, u32[]{:S(2)}, u32[]{:S(2)}) async-start(bf16[4,1,128,1024]{3,2,1,0:T(8,128)(2,1)} %copy.23), calls=%async_computation | async-start | bytes 2097152 | tf_op jit(solution)/shard_map/all_to_all | solution.py:47
  14.7 165.0 %reduce-scatter.2.cloned.1.call-start = ((), (), s32[]{:S(2)}) async-start(), calls=%async_computation.3 | async-start | bytes 5308416 | tf_op jit(solution)/shard_map/reduce_scatter | solution.py:91
Sparse Core Ops, SparseCore 0:
  83.3 96.3 reduce-scatter.1
where the time goes:
time: 272 us; the launch traced here: 271 us
  waiting for transfers between devices  96.6 us (36%)
  other arithmetic  83.6 us (31%)
  blocking collectives  33.9 us (12%)
  matrix products  16.4 us (6%)
  between operations  16.1 us (6%)
  local copies, waits for them, and re-layouts  12.4 us (5%)
  loops' own time  7.71 us (3%)
  starting transfers between devices  4.24 us (2%)
    reduce_scatter x1, waiting for transfers between devices, on_device(): owned = lax.psum_scatter(repeated, 'dp', scatter_dimension=0, tiled=True)  96.5 us
    another operation x10, other arithmetic, upper_factor(): lower_part = jnp.linalg.cholesky(matrix)  56.4 us
    all_to_all x1, blocking collectives, on_device(): lax.all_to_all(pieces, 'dp', split_axis=1, concat_axis=0, tiled=True)  20.9 us
    add x4, other arithmetic, one_source(): gram_acc + jnp.einsum('sj,sfg->jfg', table, partial_gram, precision=lax.P...  17.9 us
    unnamed x1, blocking collectives  13.1 us
    dot_general x4, matrix products, one_source(): jnp.einsum('snf,sng->sfg', hidden, hidden, preferred_element_type=jnp.flo...  8.18 us
    another operation x1, loops' own time, on_device(): lax.scan(one_source, start_gram, (arrived, slot_expert, slot_table))  7.71 us
    while x1, local copies, waits for them, and re-layouts, on_device(): lax.scan(one_source, start_gram, (arrived, slot_expert, slot_table))  6.08 us
  transfers between devices with their start and end apart: 2, of which 1 were waited for; matrix products, arithmetic and copies ran while one was open for 1% of the time, Pallas kernels for 0%

commit v1 on v0

v1 whole, which is shorter than its diff:
```python
import functools

import jax
import jax.numpy as jnp
from jax import lax
from jax.experimental import pallas as pl
from jax.experimental.pallas import tpu as pltpu
from jax.sharding import PartitionSpec as P

BLOCK = 128
RIDGE = 0.05
PANEL = 8
LANES = 128
MESH = pl.DeviceIdType.MESH
HIGHEST = lax.Precision.HIGHEST


def flip(index, bits, count):
    out = 0
    bit = 1
    while bit < count:
        digit = (index // bit) % 2
        out = out + bit * ((digit + 1) % 2 if bits & bit else digit)
        bit *= 2
    return out


def ring_place(dp, count):
    row, side = dp // 2, dp % 2
    return row + side * (count - 1 - 2 * row)


def ring_index(place, count):
    late = place // (count // 2)
    return (1 - late) * 2 * place + late * (2 * (count - 1 - place) + 1)


def gram_kernel(
    owners, replicas, experts, scale,
    expert_ref, tokens_ref, gate_hbm, up_hbm, gram_ref,
    gate_w, up_w, outgoing, arrived, id_out, id_in, id_smem, id_tile, id_ring,
    hidden, ring, w_sem, tok_sem, id_sem, small_sem, ring_sem, idr_sem,
):
    dp = lax.axis_index("dp")
    member = lax.axis_index("expert")
    width = gram_ref.shape[0]
    blocks_dev = expert_ref.shape[0]
    place = ring_place(dp, replicas)
    right = ring_index((place + 1) % replicas, replicas)
    left = ring_index((place + replicas - 1) % replicas, replicas)
    mine = dp // max(1, replicas // experts)

    load_gate = pltpu.make_async_copy(gate_hbm, gate_w, w_sem.at[0])
    load_up = pltpu.make_async_copy(up_hbm, up_w, w_sem.at[1])
    load_gate.start()
    load_up.start()

    barrier = pltpu.get_barrier_semaphore()
    for r in range(1, owners):
        pl.semaphore_signal(
            barrier, inc=1, device_id=(dp, flip(member, r, owners)), device_id_type=MESH
        )
    for side in (left, right):
        pl.semaphore_signal(barrier, inc=1, device_id=(side, member), device_id_type=MESH)

    picks = []
    for r in range(owners):
        target = flip(member, r, owners)
        index = jnp.int32(0)
        local = jnp.int32(-1)
        for b in range(blocks_dev):
            named = expert_ref[b]
            hit = named // experts == target
            index = jnp.where(hit, b, index)
            local = jnp.where(hit, named % experts, local)
        picks.append((index, local))
        id_out[r] = jnp.full((8, LANES), local, jnp.int32)
    pl.semaphore_wait(barrier, owners + 1)

    def remote(src, dst, sems, device):
        return pltpu.make_async_remote_copy(
            src_ref=src, dst_ref=dst, send_sem=sems.at[0], recv_sem=sems.at[1],
            device_id=device, device_id_type=MESH,
        )

    sent = []
    id_copies = [None]
    token_copies = [None]
    for r in range(1, owners):
        device = (dp, flip(member, r, owners))
        copy = remote(id_out.at[r], id_in.at[r], id_sem.at[r], device)
        copy.start()
        id_copies.append(copy)
        sent.append(copy)
    for r in range(1, owners):
        device = (dp, flip(member, r, owners))
        outgoing[r] = tokens_ref[picks[r][0]]
        copy = remote(outgoing.at[r], arrived.at[r], tok_sem.at[r], device)
        copy.start()
        token_copies.append(copy)
        sent.append(copy)

    locals_in = [picks[0][1]]
    for r in range(1, owners):
        id_copies[r].wait_recv()
        small = pltpu.make_async_copy(id_in.at[r], id_smem.at[r], small_sem.at[r])
        small.start()
        small.wait()
        locals_in.append(id_smem[r, 0, 0])
    for r in range(owners):
        id_tile[r * 16 : r * 16 + 16, :] = jnp.full(
            (16, LANES), locals_in[r].astype(jnp.float32), jnp.float32
        ).astype(jnp.bfloat16)

    def hops(direction, block):
        longer = replicas // 2
        first = block < owners // 2
        return longer if first == (direction == 0) else replicas - 1 - longer

    longest = replicas // 2
    peers = ((right, member), (left, member))
    id_moves = {}

    def send_ids(direction, hop):
        src = id_tile if hop == 1 else id_ring.at[direction, hop - 2]
        copy = remote(src, id_ring.at[direction, hop - 1], idr_sem.at[direction, hop - 1], peers[direction])
        copy.start()
        id_moves[direction, hop] = copy
        sent.append(copy)

    moves = {}

    def send_block(direction, hop, block):
        if hop > hops(direction, block):
            return
        src = hidden.at[block] if hop == 1 else ring.at[direction, hop - 2, block]
        copy = remote(
            src, ring.at[direction, hop - 1, block], ring_sem.at[direction, hop - 1, block],
            peers[direction],
        )
        copy.start()
        moves[direction, hop, block] = copy
        sent.append(copy)

    def add_gram(rows, ids):
        match = (ids.astype(jnp.float32) == mine.astype(jnp.float32)).astype(jnp.float32)
        match = jnp.concatenate([match] * (width // LANES), axis=1)
        kept = (rows.astype(jnp.float32) * match).astype(jnp.bfloat16)
        gram_ref[...] += lax.dot_general(
            kept, rows, (((0,), (0,)), ((), ())), preferred_element_type=jnp.float32
        )

    for direction in range(2):
        send_ids(direction, 1)
    gram_ref[...] = jnp.zeros_like(gram_ref)
    load_gate.wait()
    load_up.wait()

    events = []
    for b in range(owners):
        ready = 0.0 if b == 0 else (0.5 if b == 1 else 4.0 * (b - 1) - 0.5)
        events.append((ready, 0, -1, b))
        for direction in range(2):
            for hop in range(1, hops(direction, b) + 1):
                events.append((ready + 4.0 * hop, hop, direction, b))
    events.sort()
    for _, hop, direction, b in events:
        if hop == 0:
            if b > 0:
                token_copies[b].wait_recv()
                rows_in = arrived[b]
            else:
                rows_in = tokens_ref[picks[0][0]]
            which = jnp.maximum(locals_in[b], 0)
            gate = jnp.dot(rows_in, gate_w[which], preferred_element_type=jnp.float32)
            up = jnp.dot(rows_in, up_w[which], preferred_element_type=jnp.float32)
            hidden[b] = (gate / (1.0 + jnp.exp(-gate)) * up).astype(jnp.bfloat16)
            for d in range(2):
                send_block(d, 1, b)
            add_gram(hidden[b], id_tile[b * 16 : b * 16 + 1, :])
        else:
            if (direction, hop) in id_moves:
                id_moves.pop((direction, hop)).wait_recv()
                if hop < longest:
                    send_ids(direction, hop + 1)
            moves[direction, hop, b].wait_recv()
            send_block(direction, hop + 1, b)
            add_gram(ring[direction, hop - 1, b], id_ring[direction, hop - 1, b * 16 : b * 16 + 1, :])
    for copy in sent:
        copy.wait_send()
    row = lax.broadcasted_iota(jnp.int32, (width, width), 0)
    col = lax.broadcasted_iota(jnp.int32, (width, width), 1)
    gram_ref[...] = gram_ref[...] * scale + jnp.where(row == col, RIDGE, 0.0)


def grams(tokens, block_expert, gate_weight, up_weight):
    owners = lax.axis_size("expert")
    replicas = lax.axis_size("dp")
    experts, model, width = gate_weight.shape
    mean_rows = tokens.shape[0] * replicas // experts
    longest = replicas // 2
    bf16 = jnp.bfloat16
    vmem = pl.BlockSpec(memory_space=pltpu.VMEM)
    anywhere = pl.BlockSpec(memory_space=pl.ANY)
    dma = pltpu.SemaphoreType.DMA
    return pl.pallas_call(
        functools.partial(gram_kernel, owners, replicas, experts, 1.0 / mean_rows),
        out_shape=jax.ShapeDtypeStruct((width, width), jnp.float32),
        in_specs=[pl.BlockSpec(memory_space=pltpu.SMEM), vmem, anywhere, anywhere],
        out_specs=vmem,
        scratch_shapes=[
            pltpu.VMEM((experts, model, width), bf16),
            pltpu.VMEM((experts, model, width), bf16),
            pltpu.VMEM((owners, BLOCK, model), bf16),
            pltpu.VMEM((owners, BLOCK, model), bf16),
            pltpu.VMEM((owners, 8, LANES), jnp.int32),
            pltpu.VMEM((owners, 8, LANES), jnp.int32),
            pltpu.SMEM((owners, 8, LANES), jnp.int32),
            pltpu.VMEM((owners * 16, LANES), bf16),
            pltpu.VMEM((2, longest, owners * 16, LANES), bf16),
            pltpu.VMEM((owners, BLOCK, width), bf16),
            pltpu.VMEM((2, longest, owners, BLOCK, width), bf16),
            dma((2,)),
            dma((owners, 2)),
            dma((owners, 2)),
            dma((owners,)),
            dma((2, longest, owners, 2)),
            dma((2, longest, 2)),
        ],
        compiler_params=pltpu.CompilerParams(
            collective_id=0, has_side_effects=True, vmem_limit_bytes=52 * 1024 * 1024
        ),
        name="grams",
    )(block_expert, tokens.reshape(-1, BLOCK, model), gate_weight, up_weight)


def eliminate(tile, rows_done):
    size = tile.shape[0]
    count = size // PANEL
    halves = tile.shape[1] // LANES

    def spread(vector, lane):
        return jnp.broadcast_to(vector[:, lane : lane + 1], (PANEL, LANES))

    def down(vector, sub):
        return jnp.broadcast_to(vector[sub : sub + 1, :], (PANEL, LANES))

    groups = [
        [tile[g * PANEL : (g + 1) * PANEL, h * LANES : (h + 1) * LANES] for h in range(halves)]
        for g in range(count)
    ]
    for p in range(count):
        panel = groups[p]
        cols = [spread(panel[0], p * PANEL + k) for k in range(PANEL)]
        small = [[down(cols[k], i) if i >= k else None for k in range(PANEL)] for i in range(PANEL)]
        inverse = []
        low = [[None] * PANEL for _ in range(PANEL)]
        for k in range(PANEL):
            inv = lax.rsqrt(small[k][k])
            inverse.append(inv)
            for i in range(k + 1, PANEL):
                low[i][k] = small[i][k] * inv
            for i in range(k + 1, PANEL):
                for m in range(k + 1, i + 1):
                    small[i][m] = small[i][m] - low[i][k] * low[m][k]
        rows = []
        for k in range(PANEL):
            parts = []
            for h in range(halves):
                value = down(panel[h], k)
                for m in range(k):
                    value = value - low[k][m] * rows[m][h]
                parts.append(value * inverse[k])
            rows.append(parts)
            for h in range(halves):
                rows_done[p * PANEL + k : p * PANEL + k + 1, h * LANES : (h + 1) * LANES] = parts[h][0:1, :]
        for g in range(p + 1, count):
            weights = []
            for k in range(PANEL):
                value = spread(groups[g][0], p * PANEL + k)
                for m in range(k):
                    value = value - low[k][m] * weights[m]
                weights.append(value * inverse[k])
            for h in range(halves):
                value = groups[g][h]
                for k in range(PANEL):
                    value = value - weights[k] * rows[k][h]
                groups[g][h] = value


def factor_kernel(gram_ref, factor_ref, work, tile, done):
    width = gram_ref.shape[0]
    work[...] = gram_ref[...]
    row = lax.broadcasted_iota(jnp.int32, (LANES, LANES), 0)
    col = lax.broadcasted_iota(jnp.int32, (LANES, LANES), 1)

    def step(b, carry):
        at = pl.ds(pl.multiple_of(b * LANES, LANES), LANES)
        tile[:, :LANES] = work[at, at]
        tile[:, LANES:] = jnp.where(row == col, 1.0, 0.0)
        eliminate(tile, done)
        wide = jnp.dot(
            done[:, LANES:], work[at, :], precision=HIGHEST, preferred_element_type=jnp.float32
        )
        across = lax.broadcasted_iota(jnp.int32, wide.shape, 1) - b * LANES
        factor_ref[at, :] = jnp.where(across >= LANES, wide, 0.0)
        factor_ref[at, at] = jnp.where(row <= col, done[:, :LANES], 0.0)

        @pl.when(b + 1 < width // LANES)
        def _():
            work[...] -= lax.dot_general(
                wide, wide, (((0,), (0,)), ((), ())), precision=HIGHEST,
                preferred_element_type=jnp.float32,
            )

        return carry

    lax.fori_loop(0, width // LANES, step, 0)


def factored(gram):
    width = gram.shape[0]
    vmem = pl.BlockSpec(memory_space=pltpu.VMEM)
    return pl.pallas_call(
        factor_kernel,
        out_shape=jax.ShapeDtypeStruct((width, width), jnp.float32),
        in_specs=[vmem],
        out_specs=vmem,
        scratch_shapes=[
            pltpu.VMEM((width, width), jnp.float32),
            pltpu.VMEM((LANES, 2 * LANES), jnp.float32),
            pltpu.VMEM((LANES, 2 * LANES), jnp.float32),
        ],
        compiler_params=pltpu.CompilerParams(vmem_limit_bytes=16 * 1024 * 1024),
        name="factored",
    )(gram)


def spread_kernel(replicas, copies, factor_ref, out_ref, landed, sems):
    dp = lax.axis_index("dp")
    member = lax.axis_index("expert")
    rows = out_ref.shape[1]
    barrier = pltpu.get_barrier_semaphore()
    offsets = list(range(copies, replicas, copies))
    for r in offsets:
        pl.semaphore_signal(
            barrier, inc=1, device_id=((dp + r) % replicas, member), device_id_type=MESH
        )
    pl.semaphore_wait(barrier, len(offsets))
    sent = []
    for n, r in enumerate(offsets):
        to = (dp + r) % replicas
        copy = pltpu.make_async_remote_copy(
            src_ref=factor_ref.at[pl.ds(pl.multiple_of(to * rows, 8), rows), :],
            dst_ref=landed.at[n],
            send_sem=sems.at[n, 0],
            recv_sem=sems.at[n, 1],
            device_id=(to, member),
            device_id_type=MESH,
        )
        copy.start()
        sent.append(copy)
    out_ref[dp // copies] = factor_ref[pl.ds(pl.multiple_of(dp * rows, 8), rows), :]
    for n, r in enumerate(offsets):
        sent[n].wait_recv()
        origin = (dp + replicas - r) % replicas
        out_ref[origin // copies] = landed[n]
    for copy in sent:
        copy.wait_send()


def spread_rows(factor, experts):
    replicas = lax.axis_size("dp")
    copies = replicas // experts
    width = factor.shape[0]
    rows = width // replicas
    vmem = pl.BlockSpec(memory_space=pltpu.VMEM)
    return pl.pallas_call(
        functools.partial(spread_kernel, replicas, copies),
        out_shape=jax.ShapeDtypeStruct((experts, rows, width), jnp.float32),
        in_specs=[vmem],
        out_specs=vmem,
        scratch_shapes=[
            pltpu.VMEM((experts - 1, rows, width), jnp.float32),
            pltpu.SemaphoreType.DMA((experts - 1, 2)),
        ],
        compiler_params=pltpu.CompilerParams(
            collective_id=1, has_side_effects=True, vmem_limit_bytes=16 * 1024 * 1024
        ),
        name="spread_rows",
    )(factor)


def on_device(tokens, block_expert, gate_weight, up_weight):
    gram = grams(tokens, block_expert, gate_weight, up_weight)
    return spread_rows(factored(gram), gate_weight.shape[0])


def solution(mesh):
    placed = (
        P(("dp", "expert"), None),
        P(("dp", "expert")),
        P("expert", None, None),
        P("expert", None, None),
    )
    return jax.shard_map(
        on_device, mesh=mesh, in_specs=placed, out_specs=P("expert", "dp", None), check_vma=False
    )
```

time: 272 us -> 77.7 us (0.29)
  the two profiles are of different devices: /device:TPU:0 before, /device:TPU:15 now
where the time goes in v1:
time: 77.7 us; the launch traced here: 77.5 us
  Pallas kernels  74.8 us (96%)
  local copies, waits for them, and re-layouts  2.7 us (3%)
    pallas_call x1, Pallas kernels, grams(): pl.pallas_call(functools.partial(gram_kernel, owners, replicas, experts,...  41.8 us
    pallas_call x1, Pallas kernels, spread_rows(): pl.pallas_call(functools.partial(spread_kernel, replicas, copies), out_sh...  17.6 us
    pallas_call x1, Pallas kernels, factored(): pl.pallas_call(factor_kernel, out_shape=jax.ShapeDtypeStruct((width, widt...  15.4 us
    unnamed x5, local copies, waits for them, and re-layouts  2.7 us

profile of v1, /device:TPU:15, one launch (start us, length us, event | category | flops | bytes accessed | tf_op | source)
XLA Modules:
  0.0 77.5 jit_solution(13464217566867934776)
XLA Ops:
  0.0 0.0 copy-start
  0.0 1.2 %copy-done = bf16[512,1024]{1,0:T(8,128)(2,1)S(1)} copy-done((bf16[512,1024]{1,0:T(8,128)(2,1)S(1)}, bf16[512,1024]{1,0:T(8,128)(2,1)}, u32[]{:S(2)}) %copy-start) | copy-done | bytes 1048600
  1.2 0.0 copy-start.1
  1.2 0.7 copy-done.1
  1.9 41.8 %grams.1.gram_ref = f32[384,384]{1,0:T(8,128)S(1)} custom-call(s32[4]{0:T(128)S(1)} %copy-done.1, bf16[4,128,1024]{2,1,0:T(8,128)(2,1)S(1)} %bitcast.1, bf16[8,1024,384]{2,1,0:T(8,128)(2,1)} %gate_hbm.1, bf16[8,1024,384]{2,1,0:T(8,128)(2,1)} %up_hbm.1), custom_call_target="tpu_custom_call" | custom-call | tf_op jit(solution)/shard_map/grams/pallas_call | solution.py:206
  43.7 15.4 %factored.1.factor_ref = f32[384,384]{1,0:T(8,128)S(1)} custom-call(f32[384,384]{1,0:T(8,128)S(1)} %grams.1.gram_ref), custom_call_target="tpu_custom_call" | custom-call | tf_op jit(solution)/shard_map/factored/pallas_call | solution.py:324
  59.1 17.6 %spread_rows.1 = f32[8,48,384]{2,1,0:T(8,128)S(1)} custom-call(f32[384,384]{1,0:T(8,128)S(1)} %factored.1.factor_ref), custom_call_target="tpu_custom_call" | custom-call | tf_op jit(solution)/shard_map/spread_rows/pallas_call | solution.py:378
  76.7 0.8 %copy.6 = f32[8,48,384]{2,1,0:T(8,128)} copy(f32[8,48,384]{2,1,0:T(8,128)S(1)} %spread_rows.1) | data formatting | bytes 1179648
Async XLA Ops:
  0.0 1.2 %copy-start = (bf16[512,1024]{1,0:T(8,128)(2,1)S(1)}, bf16[512,1024]{1,0:T(8,128)(2,1)}, u32[]{:S(2)}) copy-start(bf16[512,1024]{1,0:T(8,128)(2,1)} %param.4) | copy-start | bytes 3145732
  1.2 0.7 copy-start.1

commit v2 on v1

--- a/solution.py
+++ b/solution.py
@@ -1,4 +1,5 @@
 import functools
+import heapq
 
 import jax
 import jax.numpy as jnp
@@ -25,6 +26,10 @@
     return out
 
 
+def ready_time(block):
+    return (0.0, 0.7, 6.0, 7.5)[block] if block < 4 else 2.0 * block
+
+
 def ring_place(dp, count):
     row, side = dp // 2, dp % 2
     return row + side * (count - 1 - 2 * row)
@@ -37,8 +42,8 @@
 
 def gram_kernel(
     owners, replicas, experts, scale,
-    expert_ref, tokens_ref, gate_hbm, up_hbm, gram_ref,
-    gate_w, up_w, outgoing, arrived, id_out, id_in, id_smem, id_tile, id_ring,
+    expert_ref, tokens_hbm, gate_hbm, up_hbm, gram_ref,
+    tokens_ref, gate_w, up_w, outgoing, arrived, id_out, id_in, id_smem, id_tile, id_ring,
     hidden, ring, w_sem, tok_sem, id_sem, small_sem, ring_sem, idr_sem,
 ):
     dp = lax.axis_index("dp")
@@ -52,6 +57,8 @@
 
     load_gate = pltpu.make_async_copy(gate_hbm, gate_w, w_sem.at[0])
     load_up = pltpu.make_async_copy(up_hbm, up_w, w_sem.at[1])
+    load_tokens = pltpu.make_async_copy(tokens_hbm, tokens_ref, w_sem.at[2])
+    load_tokens.start()
     load_gate.start()
     load_up.start()
 
@@ -92,6 +99,7 @@
         copy.start()
         id_copies.append(copy)
         sent.append(copy)
+    load_tokens.wait()
     for r in range(1, owners):
         device = (dp, flip(member, r, owners))
         outgoing[r] = tokens_ref[picks[r][0]]
@@ -142,13 +150,18 @@
         moves[direction, hop, block] = copy
         sent.append(copy)
 
-    def add_gram(rows, ids):
-        match = (ids.astype(jnp.float32) == mine.astype(jnp.float32)).astype(jnp.float32)
-        match = jnp.concatenate([match] * (width // LANES), axis=1)
-        kept = (rows.astype(jnp.float32) * match).astype(jnp.bfloat16)
-        gram_ref[...] += lax.dot_general(
-            kept, rows, (((0,), (0,)), ((), ())), preferred_element_type=jnp.float32
-        )
+    def add_gram(parts):
+        kept = []
+        for rows, ids in parts:
+            match = (ids.astype(jnp.float32) == mine.astype(jnp.float32)).astype(jnp.float32)
+            match = jnp.concatenate([match] * (width // LANES), axis=1)
+            kept.append((rows.astype(jnp.float32) * match).astype(jnp.bfloat16))
+        kept = jnp.concatenate(kept, axis=0)
+        for at in range(0, width, LANES):
+            gram_ref[at : at + LANES, at:] += lax.dot_general(
+                kept[:, at : at + LANES], kept[:, at:], (((0,), (0,)), ((), ())),
+                preferred_element_type=jnp.float32,
+            )
 
     for direction in range(2):
         send_ids(direction, 1)
@@ -156,15 +169,21 @@
     load_gate.wait()
     load_up.wait()
 
-    events = []
-    for b in range(owners):
-        ready = 0.0 if b == 0 else (0.5 if b == 1 else 4.0 * (b - 1) - 0.5)
-        events.append((ready, 0, -1, b))
-        for direction in range(2):
-            for hop in range(1, hops(direction, b) + 1):
-                events.append((ready + 4.0 * hop, hop, direction, b))
-    events.sort()
-    for _, hop, direction, b in events:
+    queue = [(ready_time(b), 0, b) for b in range(owners)]
+    order = []
+    free = [0.0, 0.0]
+    while queue:
+        now, hop, b = heapq.heappop(queue)
+        order.append((hop, b))
+        landed = []
+        for d in range(2):
+            if hop < hops(d, b):
+                free[d] = max(now, free[d]) + 2.0
+                landed.append(free[d])
+        if landed:
+            heapq.heappush(queue, (max(landed), hop + 1, b))
+
+    for hop, b in order:
         if hop == 0:
             if b > 0:
                 token_copies[b].wait_recv()
@@ -177,15 +196,20 @@
             hidden[b] = (gate / (1.0 + jnp.exp(-gate)) * up).astype(jnp.bfloat16)
             for d in range(2):
                 send_block(d, 1, b)
-            add_gram(hidden[b], id_tile[b * 16 : b * 16 + 1, :])
+            add_gram([(hidden[b], id_tile[b * 16 : b * 16 + 1, :])])
         else:
-            if (direction, hop) in id_moves:
-                id_moves.pop((direction, hop)).wait_recv()
-                if hop < longest:
-                    send_ids(direction, hop + 1)
-            moves[direction, hop, b].wait_recv()
-            send_block(direction, hop + 1, b)
-            add_gram(ring[direction, hop - 1, b], id_ring[direction, hop - 1, b * 16 : b * 16 + 1, :])
+            parts = []
+            for d in range(2):
+                if hop > hops(d, b):
+                    continue
+                if (d, hop) in id_moves:
+                    id_moves.pop((d, hop)).wait_recv()
+                    if hop < longest:
+                        send_ids(d, hop + 1)
+                moves[d, hop, b].wait_recv()
+                send_block(d, hop + 1, b)
+                parts.append((d, hop - 1))
+            add_gram([(ring[d, h, b], id_ring[d, h, b * 16 : b * 16 + 1, :]) for d, h in parts])
     for copy in sent:
         copy.wait_send()
     row = lax.broadcasted_iota(jnp.int32, (width, width), 0)
@@ -206,9 +230,10 @@
     return pl.pallas_call(
         functools.partial(gram_kernel, owners, replicas, experts, 1.0 / mean_rows),
         out_shape=jax.ShapeDtypeStruct((width, width), jnp.float32),
-        in_specs=[pl.BlockSpec(memory_space=pltpu.SMEM), vmem, anywhere, anywhere],
+        in_specs=[pl.BlockSpec(memory_space=pltpu.SMEM), anywhere, anywhere, anywhere],
         out_specs=vmem,
         scratch_shapes=[
+            pltpu.VMEM((tokens.shape[0] // BLOCK, BLOCK, model), bf16),
             pltpu.VMEM((experts, model, width), bf16),
             pltpu.VMEM((experts, model, width), bf16),
             pltpu.VMEM((owners, BLOCK, model), bf16),
@@ -220,7 +245,7 @@
             pltpu.VMEM((2, longest, owners * 16, LANES), bf16),
             pltpu.VMEM((owners, BLOCK, width), bf16),
             pltpu.VMEM((2, longest, owners, BLOCK, width), bf16),
-            dma((2,)),
+            dma((3,)),
             dma((owners, 2)),
             dma((owners, 2)),
             dma((owners,)),

time: 77.7 us -> 78.3 us (level)
  the two profiles are of different devices: /device:TPU:15 before, /device:TPU:0 now
where the time goes in v2:
time: 78.3 us; the launch traced here: 76.7 us
  Pallas kernels  74 us (95%)
  local copies, waits for them, and re-layouts  2.7 us (3%)
    pallas_call x1, Pallas kernels, grams(): pl.pallas_call(functools.partial(gram_kernel, owners, replicas, experts,...  45.6 us
    pallas_call x1, Pallas kernels, factored(): pl.pallas_call(factor_kernel, out_shape=jax.ShapeDtypeStruct((width, widt...  15.4 us
    pallas_call x1, Pallas kernels, spread_rows(): pl.pallas_call(functools.partial(spread_kernel, replicas, copies), out_sh...  13 us
    unnamed x5, local copies, waits for them, and re-layouts  2.7 us

profile of v2, /device:TPU:0, one launch (start us, length us, event | category | flops | bytes accessed | tf_op | source)
XLA Modules:
  0.0 76.7 jit_solution(7252395298359682877)
XLA Ops:
  0.0 0.0 copy-start
  0.0 1.2 %copy-done = bf16[512,1024]{1,0:T(8,128)(2,1)S(1)} copy-done((bf16[512,1024]{1,0:T(8,128)(2,1)S(1)}, bf16[512,1024]{1,0:T(8,128)(2,1)}, u32[]{:S(2)}) %copy-start) | copy-done | bytes 1048600
  1.2 0.0 copy-start.1
  1.2 0.7 copy-done.1
  1.9 45.6 %grams.1.gram_ref = f32[384,384]{1,0:T(8,128)S(1)} custom-call(s32[4]{0:T(128)S(1)} %copy-done.1, bf16[4,128,1024]{2,1,0:T(8,128)(2,1)S(1)} %bitcast.1, bf16[8,1024,384]{2,1,0:T(8,128)(2,1)} %gate_hbm.1, bf16[8,1024,384]{2,1,0:T(8,128)(2,1)} %up_hbm.1), custom_call_target="tpu_custom_call" | custom-call | tf_op jit(solution)/shard_map/grams/pallas_call | solution.py:230
  47.5 15.4 %factored.1.factor_ref = f32[384,384]{1,0:T(8,128)S(1)} custom-call(f32[384,384]{1,0:T(8,128)S(1)} %grams.1.gram_ref), custom_call_target="tpu_custom_call" | custom-call | tf_op jit(solution)/shard_map/factored/pallas_call | solution.py:349
  62.9 13.0 %spread_rows.1 = f32[8,48,384]{2,1,0:T(8,128)S(1)} custom-call(f32[384,384]{1,0:T(8,128)S(1)} %factored.1.factor_ref), custom_call_target="tpu_custom_call" | custom-call | tf_op jit(solution)/shard_map/spread_rows/pallas_call | solution.py:403
  75.9 0.8 %copy.6 = f32[8,48,384]{2,1,0:T(8,128)} copy(f32[8,48,384]{2,1,0:T(8,128)S(1)} %spread_rows.1) | data formatting | bytes 1179648
Async XLA Ops:
  0.0 1.2 %copy-start = (bf16[512,1024]{1,0:T(8,128)(2,1)S(1)}, bf16[512,1024]{1,0:T(8,128)(2,1)}, u32[]{:S(2)}) copy-start(bf16[512,1024]{1,0:T(8,128)(2,1)} %param.4) | copy-start | bytes 3145732
  1.2 0.7 copy-start.1

commit v3 on v2

--- a/solution.py
+++ b/solution.py
@@ -92,7 +92,6 @@
 
     sent = []
     id_copies = [None]
-    token_copies = [None]
     for r in range(1, owners):
         device = (dp, flip(member, r, owners))
         copy = remote(id_out.at[r], id_in.at[r], id_sem.at[r], device)
@@ -100,26 +99,34 @@
         id_copies.append(copy)
         sent.append(copy)
     load_tokens.wait()
-    for r in range(1, owners):
+    token_copies = [None] * owners
+    for r in list(range(2, owners)) + [1]:
         device = (dp, flip(member, r, owners))
         outgoing[r] = tokens_ref[picks[r][0]]
         copy = remote(outgoing.at[r], arrived.at[r], tok_sem.at[r], device)
         copy.start()
-        token_copies.append(copy)
+        token_copies[r] = copy
         sent.append(copy)
 
     locals_in = [picks[0][1]]
-    for r in range(1, owners):
-        id_copies[r].wait_recv()
-        small = pltpu.make_async_copy(id_in.at[r], id_smem.at[r], small_sem.at[r])
-        small.start()
-        small.wait()
-        locals_in.append(id_smem[r, 0, 0])
-    for r in range(owners):
+
+    def keep_id(r):
         id_tile[r * 16 : r * 16 + 16, :] = jnp.full(
             (16, LANES), locals_in[r].astype(jnp.float32), jnp.float32
         ).astype(jnp.bfloat16)
 
+    def collect_ids():
+        small = [None]
+        for r in range(1, owners):
+            id_copies[r].wait_recv()
+            small.append(pltpu.make_async_copy(id_in.at[r], id_smem.at[r], small_sem.at[r]))
+            small[r].start()
+        for r in range(1, owners):
+            small[r].wait()
+            locals_in.append(id_smem[r, 0, 0])
+            keep_id(r)
+
+    keep_id(0)
     def hops(direction, block):
         longer = replicas // 2
         first = block < owners // 2
@@ -163,11 +170,7 @@
                 preferred_element_type=jnp.float32,
             )
 
-    for direction in range(2):
-        send_ids(direction, 1)
     gram_ref[...] = jnp.zeros_like(gram_ref)
-    load_gate.wait()
-    load_up.wait()
 
     queue = [(ready_time(b), 0, b) for b in range(owners)]
     order = []
@@ -191,11 +194,19 @@
             else:
                 rows_in = tokens_ref[picks[0][0]]
             which = jnp.maximum(locals_in[b], 0)
+            if b == 0:
+                load_gate.wait()
             gate = jnp.dot(rows_in, gate_w[which], preferred_element_type=jnp.float32)
+            if b == 0:
+                load_up.wait()
             up = jnp.dot(rows_in, up_w[which], preferred_element_type=jnp.float32)
             hidden[b] = (gate / (1.0 + jnp.exp(-gate)) * up).astype(jnp.bfloat16)
             for d in range(2):
                 send_block(d, 1, b)
+            if b == 0:
+                collect_ids()
+                for d in range(2):
+                    send_ids(d, 1)
             add_gram([(hidden[b], id_tile[b * 16 : b * 16 + 1, :])])
         else:
             parts = []
@@ -313,7 +324,7 @@
                 groups[g][h] = value
 
 
-def factor_kernel(gram_ref, factor_ref, work, tile, done):
+def factor_kernel(gram_ref, rows_ref, factor_ref, work, tile, done):
     width = gram_ref.shape[0]
     work[...] = gram_ref[...]
     row = lax.broadcasted_iota(jnp.int32, (LANES, LANES), 0)
@@ -341,17 +352,26 @@
         return carry
 
     lax.fori_loop(0, width // LANES, step, 0)
-
-
-def factored(gram):
+    replicas, padded, _ = rows_ref.shape
+    rows = width // replicas
+    for d in range(replicas):
+        part = factor_ref[d * rows : (d + 1) * rows, :]
+        if padded > rows:
+            part = jnp.concatenate([part, jnp.zeros((padded - rows, width), part.dtype)], axis=0)
+        rows_ref[d] = part.astype(rows_ref.dtype)
+
+
+def factored(gram, replicas):
     width = gram.shape[0]
+    padded = -(-(width // replicas) // 16) * 16
     vmem = pl.BlockSpec(memory_space=pltpu.VMEM)
     return pl.pallas_call(
         factor_kernel,
-        out_shape=jax.ShapeDtypeStruct((width, width), jnp.float32),
+        out_shape=jax.ShapeDtypeStruct((replicas, padded, width), jnp.bfloat16),
         in_specs=[vmem],
         out_specs=vmem,
         scratch_shapes=[
+            pltpu.VMEM((width, width), jnp.float32),
             pltpu.VMEM((width, width), jnp.float32),
             pltpu.VMEM((LANES, 2 * LANES), jnp.float32),
             pltpu.VMEM((LANES, 2 * LANES), jnp.float32),
@@ -364,7 +384,6 @@
 def spread_kernel(replicas, copies, factor_ref, out_ref, landed, sems):
     dp = lax.axis_index("dp")
     member = lax.axis_index("expert")
-    rows = out_ref.shape[1]
     barrier = pltpu.get_barrier_semaphore()
     offsets = list(range(copies, replicas, copies))
     for r in offsets:
@@ -376,7 +395,7 @@
     for n, r in enumerate(offsets):
         to = (dp + r) % replicas
         copy = pltpu.make_async_remote_copy(
-            src_ref=factor_ref.at[pl.ds(pl.multiple_of(to * rows, 8), rows), :],
+            src_ref=factor_ref.at[to],
             dst_ref=landed.at[n],
             send_sem=sems.at[n, 0],
             recv_sem=sems.at[n, 1],
@@ -385,7 +404,7 @@
         )
         copy.start()
         sent.append(copy)
-    out_ref[dp // copies] = factor_ref[pl.ds(pl.multiple_of(dp * rows, 8), rows), :]
+    out_ref[dp // copies] = factor_ref[dp]
     for n, r in enumerate(offsets):
         sent[n].wait_recv()
         origin = (dp + replicas - r) % replicas
@@ -395,18 +414,16 @@
 
 
 def spread_rows(factor, experts):
-    replicas = lax.axis_size("dp")
-    copies = replicas // experts
-    width = factor.shape[0]
+    replicas, padded, width = factor.shape
     rows = width // replicas
     vmem = pl.BlockSpec(memory_space=pltpu.VMEM)
-    return pl.pallas_call(
-        functools.partial(spread_kernel, replicas, copies),
-        out_shape=jax.ShapeDtypeStruct((experts, rows, width), jnp.float32),
+    out = pl.pallas_call(
+        functools.partial(spread_kernel, replicas, replicas // experts),
+        out_shape=jax.ShapeDtypeStruct((experts, padded, width), factor.dtype),
         in_specs=[vmem],
         out_specs=vmem,
         scratch_shapes=[
-            pltpu.VMEM((experts - 1, rows, width), jnp.float32),
+            pltpu.VMEM((experts - 1, padded, width), factor.dtype),
             pltpu.SemaphoreType.DMA((experts - 1, 2)),
         ],
         compiler_params=pltpu.CompilerParams(
@@ -414,11 +431,12 @@
         ),
         name="spread_rows",
     )(factor)
+    return out[:, :rows].astype(jnp.float32)
 
 
 def on_device(tokens, block_expert, gate_weight, up_weight):
     gram = grams(tokens, block_expert, gate_weight, up_weight)
-    return spread_rows(factored(gram), gate_weight.shape[0])
+    return spread_rows(factored(gram, lax.axis_size("dp")), gate_weight.shape[0])
 
 
 def solution(mesh):

time: 78.3 us -> 72.8 us (0.930); the launches traced: 76.7 us -> 72.7 us
  Pallas kernels: 74 us -> 69.9 us
  other arithmetic: 0 us -> 0.85 us
  local copies, waits for them, and re-layouts: 2.7 us -> 1.88 us
    pallas_call x2, Pallas kernels: 28.4 us -> 24.9 us  [the longest x1 15.4 us: factored(): pl.pallas_call(factor_kernel, out_shape=jax.ShapeDtypeStruct((replicas, p...]
    convert_element_type x0 -> x1, other arithmetic: none -> 0.85 us  [spread_rows(): return out[:, :rows].astype(jnp.float32)]
    unnamed x5 -> x4, local copies, waits for them, and re-layouts: 2.7 us -> 1.88 us
where the time goes in v3:
time: 72.8 us; the launch traced here: 72.7 us
  Pallas kernels  69.9 us (96%)
  local copies, waits for them, and re-layouts  1.88 us (3%)
  other arithmetic  0.85 us (1%)
    pallas_call x1, Pallas kernels, grams(): pl.pallas_call(functools.partial(gram_kernel, owners, replicas, experts,...  45 us
    pallas_call x1, Pallas kernels, factored(): pl.pallas_call(factor_kernel, out_shape=jax.ShapeDtypeStruct((replicas, p...  15.4 us
    pallas_call x1, Pallas kernels, spread_rows(): pl.pallas_call(functools.partial(spread_kernel, replicas, replicas // exp...  9.45 us
    unnamed x4, local copies, waits for them, and re-layouts  1.88 us

profile of v3, /device:TPU:0, one launch (start us, length us, event | category | flops | bytes accessed | tf_op | source)
XLA Modules:
  0.0 72.7 jit_solution(10928615076993841058)
XLA Ops:
  0.0 0.0 copy-start
  0.0 1.2 %copy-done = bf16[512,1024]{1,0:T(8,128)(2,1)S(1)} copy-done((bf16[512,1024]{1,0:T(8,128)(2,1)S(1)}, bf16[512,1024]{1,0:T(8,128)(2,1)}, u32[]{:S(2)}) %copy-start) | copy-done | bytes 1048600
  1.2 0.0 copy-start.1
  1.2 0.7 copy-done.1
  1.9 45.0 %grams.1.gram_ref = f32[384,384]{1,0:T(8,128)S(1)} custom-call(s32[4]{0:T(128)S(1)} %copy-done.1, bf16[4,128,1024]{2,1,0:T(8,128)(2,1)S(1)} %bitcast.1, bf16[8,1024,384]{2,1,0:T(8,128)(2,1)} %gate_hbm.1, bf16[8,1024,384]{2,1,0:T(8,128)(2,1)} %up_hbm.1), custom_call_target="tpu_custom_call" | custom-call | tf_op jit(solution)/shard_map/grams/pallas_call | solution.py:241
  46.9 15.4 %factored.1.factor_ref = bf16[8,48,384]{2,1,0:T(8,128)(2,1)S(1)} custom-call(f32[384,384]{1,0:T(8,128)S(1)} %grams.1.gram_ref), custom_call_target="tpu_custom_call" | custom-call | tf_op jit(solution)/shard_map/factored/pallas_call | solution.py:368
  62.4 9.4 %spread_rows.1 = bf16[8,48,384]{2,1,0:T(8,128)(2,1)S(1)} custom-call(bf16[8,48,384]{2,1,0:T(8,128)(2,1)S(1)} %factored.1.factor_ref), custom_call_target="tpu_custom_call" | custom-call | tf_op jit(solution)/shard_map/spread_rows/pallas_call | solution.py:420
  71.8 0.9 %convert_element_type.3 = f32[8,48,384]{2,1,0:T(8,128)} convert(bf16[8,48,384]{2,1,0:T(8,128)(2,1)S(1)} %spread_rows.1) | non-fusion elementwise | flops 147456 | bytes 884736 | tf_op jit(solution)/shard_map/convert_element_type | solution.py:434
Async XLA Ops:
  0.0 1.2 %copy-start = (bf16[512,1024]{1,0:T(8,128)(2,1)S(1)}, bf16[512,1024]{1,0:T(8,128)(2,1)}, u32[]{:S(2)}) copy-start(bf16[512,1024]{1,0:T(8,128)(2,1)} %param.4) | copy-start | bytes 3145732
  1.2 0.7 copy-start.1

commit v4 on v3

--- a/solution.py
+++ b/solution.py
@@ -324,11 +324,50 @@
                 groups[g][h] = value
 
 
-def factor_kernel(gram_ref, rows_ref, factor_ref, work, tile, done):
+def row_pieces(width, rows):
+    pieces = []
+    for holder in range(width // rows):
+        start, end, which = holder * rows, (holder + 1) * rows, 0
+        while start < end:
+            stop = min(end, (start // LANES + 1) * LANES)
+            pieces.append((start // LANES, holder, start, stop, which))
+            start, which = stop, which + 1
+    return pieces
+
+
+def factor_kernel(replicas, copies, gram_ref, out_ref, factor, work, tile, done, landed, send_sem, recv_sem):
+    dp = lax.axis_index("dp")
+    member = lax.axis_index("expert")
     width = gram_ref.shape[0]
+    rows = width // replicas
+    pieces = row_pieces(width, rows)
+
+    barrier = pltpu.get_barrier_semaphore()
+    offsets = list(range(copies, replicas, copies))
+    for r in offsets:
+        pl.semaphore_signal(
+            barrier, inc=1, device_id=((dp + r) % replicas, member), device_id_type=MESH
+        )
+
+    def piece_copy(block, holder, start, stop, which, origin):
+        first = start - holder * rows
+        return pltpu.make_async_remote_copy(
+            src_ref=factor.at[start:stop, block * LANES :],
+            dst_ref=landed.at[origin, first : first + stop - start, block * LANES :],
+            send_sem=send_sem.at[holder, which],
+            recv_sem=recv_sem.at[origin, which],
+            device_id=(holder, member),
+            device_id_type=MESH,
+        )
+
+    def serves(holder):
+        return jnp.logical_and(dp % copies == holder % copies, dp != holder)
+
     work[...] = gram_ref[...]
+    out_ref[...] = jnp.zeros_like(out_ref)
     row = lax.broadcasted_iota(jnp.int32, (LANES, LANES), 0)
     col = lax.broadcasted_iota(jnp.int32, (LANES, LANES), 1)
+    pl.semaphore_wait(barrier, len(offsets))
 
     def step(b, carry):
         at = pl.ds(pl.multiple_of(b * LANES, LANES), LANES)
@@ -339,8 +378,13 @@
             done[:, LANES:], work[at, :], precision=HIGHEST, preferred_element_type=jnp.float32
         )
         across = lax.broadcasted_iota(jnp.int32, wide.shape, 1) - b * LANES
-        factor_ref[at, :] = jnp.where(across >= LANES, wide, 0.0)
-        factor_ref[at, at] = jnp.where(row <= col, done[:, :LANES], 0.0)
+        factor[at, :] = jnp.where(across >= LANES, wide, 0.0)
+        factor[at, at] = jnp.where(row <= col, done[:, :LANES], 0.0)
+        for piece in pieces:
+
+            @pl.when(jnp.logical_and(b == piece[0], serves(piece[1])))
+            def _():
+                piece_copy(*piece, dp // copies).start()
 
         @pl.when(b + 1 < width // LANES)
         def _():
@@ -352,22 +396,36 @@
         return carry
 
     lax.fori_loop(0, width // LANES, step, 0)
-    replicas, padded, _ = rows_ref.shape
+
+    out_ref[dp // copies] = factor[pl.ds(pl.multiple_of(dp * rows, 8), rows), :]
+    for piece in pieces:
+        block, holder, start, stop, which = piece
+        first = start - holder * rows
+
+        @pl.when(dp == holder)
+        def _():
+            for origin in range(replicas // copies):
+                if origin != holder // copies:
+                    piece_copy(*piece, origin).wait_recv()
+                    part = (origin, slice(first, first + stop - start), slice(block * LANES, width))
+                    out_ref[part] = landed[part]
+
+    for piece in pieces:
+
+        @pl.when(serves(piece[1]))
+        def _():
+            piece_copy(*piece, dp // copies).wait_send()
+
+
+def factored_rows(gram, experts):
+    width = gram.shape[0]
+    replicas = lax.axis_size("dp")
     rows = width // replicas
-    for d in range(replicas):
-        part = factor_ref[d * rows : (d + 1) * rows, :]
-        if padded > rows:
-            part = jnp.concatenate([part, jnp.zeros((padded - rows, width), part.dtype)], axis=0)
-        rows_ref[d] = part.astype(rows_ref.dtype)
-
-
-def factored(gram, replicas):
-    width = gram.shape[0]
-    padded = -(-(width // replicas) // 16) * 16
+    most = 1 + max(piece[4] for piece in row_pieces(width, rows))
     vmem = pl.BlockSpec(memory_space=pltpu.VMEM)
     return pl.pallas_call(
-        factor_kernel,
-        out_shape=jax.ShapeDtypeStruct((replicas, padded, width), jnp.bfloat16),
+        functools.partial(factor_kernel, replicas, replicas // experts),
+        out_shape=jax.ShapeDtypeStruct((experts, rows, width), jnp.float32),
         in_specs=[vmem],
         out_specs=vmem,
         scratch_shapes=[
@@ -375,68 +433,20 @@
             pltpu.VMEM((width, width), jnp.float32),
             pltpu.VMEM((LANES, 2 * LANES), jnp.float32),
             pltpu.VMEM((LANES, 2 * LANES), jnp.float32),
-        ],
-        compiler_params=pltpu.CompilerParams(vmem_limit_bytes=16 * 1024 * 1024),
-        name="factored",
-    )(gram)
-
-
-def spread_kernel(replicas, copies, factor_ref, out_ref, landed, sems):
-    dp = lax.axis_index("dp")
-    member = lax.axis_index("expert")
-    barrier = pltpu.get_barrier_semaphore()
-    offsets = list(range(copies, replicas, copies))
-    for r in offsets:
-        pl.semaphore_signal(
-            barrier, inc=1, device_id=((dp + r) % replicas, member), device_id_type=MESH
-        )
-    pl.semaphore_wait(barrier, len(offsets))
-    sent = []
-    for n, r in enumerate(offsets):
-        to = (dp + r) % replicas
-        copy = pltpu.make_async_remote_copy(
-            src_ref=factor_ref.at[to],
-            dst_ref=landed.at[n],
-            send_sem=sems.at[n, 0],
-            recv_sem=sems.at[n, 1],
-            device_id=(to, member),
-            device_id_type=MESH,
-        )
-        copy.start()
-        sent.append(copy)
-    out_ref[dp // copies] = factor_ref[dp]
-    for n, r in enumerate(offsets):
-        sent[n].wait_recv()
-        origin = (dp + replicas - r) % replicas
-        out_ref[origin // copies] = landed[n]
-    for copy in sent:
-        copy.wait_send()
-
-
-def spread_rows(factor, experts):
-    replicas, padded, width = factor.shape
-    rows = width // replicas
-    vmem = pl.BlockSpec(memory_space=pltpu.VMEM)
-    out = pl.pallas_call(
-        functools.partial(spread_kernel, replicas, replicas // experts),
-        out_shape=jax.ShapeDtypeStruct((experts, padded, width), factor.dtype),
-        in_specs=[vmem],
-        out_specs=vmem,
-        scratch_shapes=[
-            pltpu.VMEM((experts - 1, padded, width), factor.dtype),
-            pltpu.SemaphoreType.DMA((experts - 1, 2)),
+            pltpu.VMEM((experts, rows, width), jnp.float32),
+            pltpu.SemaphoreType.DMA((replicas, most)),
+            pltpu.SemaphoreType.DMA((experts, most)),
         ],
         compiler_params=pltpu.CompilerParams(
             collective_id=1, has_side_effects=True, vmem_limit_bytes=16 * 1024 * 1024
         ),
-        name="spread_rows",
-    )(factor)
-    return out[:, :rows].astype(jnp.float32)
+        name="factored_rows",
+    )(gram)
 
 
 def on_device(tokens, block_expert, gate_weight, up_weight):
     gram = grams(tokens, block_expert, gate_weight, up_weight)
-    return spread_rows(factored(gram, lax.axis_size("dp")), gate_weight.shape[0])
+    return factored_rows(gram, gate_weight.shape[0])
 
 
 def solution(mesh):

time: 72.8 us -> 70.6 us (0.970)
  Pallas kernels: 69.9 us -> 67.7 us
  other arithmetic: 0.85 us -> 0 us
  local copies, waits for them, and re-layouts: 1.88 us -> 2.7 us
    pallas_call x2 -> x1, Pallas kernels: 24.9 us -> 22.7 us  [factored_rows(): pl.pallas_call(functools.partial(factor_kernel, replicas, replicas // exp...]
    convert_element_type x1 -> x0, other arithmetic: 0.85 us -> none  [spread_rows(): return out[:, :rows].astype(jnp.float32)]
    unnamed x4 -> x5, local copies, waits for them, and re-layouts: 1.88 us -> 2.7 us
where the time goes in v4:
time: 70.6 us; the launch traced here: 70.4 us
  Pallas kernels  67.7 us (96%)
  local copies, waits for them, and re-layouts  2.7 us (4%)
    pallas_call x1, Pallas kernels, grams(): pl.pallas_call(functools.partial(gram_kernel, owners, replicas, experts,...  45 us
    pallas_call x1, Pallas kernels, factored_rows(): pl.pallas_call(functools.partial(factor_kernel, replicas, replicas // exp...  22.7 us
    unnamed x5, local copies, waits for them, and re-layouts  2.7 us

profile of v4, /device:TPU:0, one launch (start us, length us, event | category | flops | bytes accessed | tf_op | source)
XLA Modules:
  0.0 70.4 jit_solution(8638794371160576100)
XLA Ops:
  0.0 0.0 copy-start
  0.0 1.2 %copy-done = bf16[512,1024]{1,0:T(8,128)(2,1)S(1)} copy-done((bf16[512,1024]{1,0:T(8,128)(2,1)S(1)}, bf16[512,1024]{1,0:T(8,128)(2,1)}, u32[]{:S(2)}) %copy-start) | copy-done | bytes 1048600
  1.2 0.0 copy-start.1
  1.2 0.7 copy-done.1
  1.9 45.0 %grams.1.gram_ref = f32[384,384]{1,0:T(8,128)S(1)} custom-call(s32[4]{0:T(128)S(1)} %copy-done.1, bf16[4,128,1024]{2,1,0:T(8,128)(2,1)S(1)} %bitcast.1, bf16[8,1024,384]{2,1,0:T(8,128)(2,1)} %gate_hbm.1, bf16[8,1024,384]{2,1,0:T(8,128)(2,1)} %up_hbm.1), custom_call_target="tpu_custom_call" | custom-call | tf_op jit(solution)/shard_map/grams/pallas_call | solution.py:241
  46.9 22.7 %factored_rows.1 = f32[8,48,384]{2,1,0:T(8,128)S(1)} custom-call(f32[384,384]{1,0:T(8,128)S(1)} %grams.1.gram_ref), custom_call_target="tpu_custom_call" | custom-call | tf_op jit(solution)/shard_map/factored_rows/pallas_call | solution.py:426
  69.6 0.8 %copy.6 = f32[8,48,384]{2,1,0:T(8,128)} copy(f32[8,48,384]{2,1,0:T(8,128)S(1)} %factored_rows.1) | data formatting | bytes 1179648
Async XLA Ops:
  0.0 1.2 %copy-start = (bf16[512,1024]{1,0:T(8,128)(2,1)S(1)}, bf16[512,1024]{1,0:T(8,128)(2,1)}, u32[]{:S(2)}) copy-start(bf16[512,1024]{1,0:T(8,128)(2,1)} %param.4) | copy-start | bytes 3145732
  1.2 0.7 copy-start.1

commit v5 on v4

--- a/solution.py
+++ b/solution.py
@@ -27,7 +27,7 @@
 
 
 def ready_time(block):
-    return (0.0, 0.7, 6.0, 7.5)[block] if block < 4 else 2.0 * block
+    return (0.0, 0.7, 9.0, 10.0)[block] if block < 4 else 2.0 * block
 
 
 def ring_place(dp, count):
@@ -110,10 +110,13 @@
 
     locals_in = [picks[0][1]]
 
-    def keep_id(r):
-        id_tile[r * 16 : r * 16 + 16, :] = jnp.full(
-            (16, LANES), locals_in[r].astype(jnp.float32), jnp.float32
-        ).astype(jnp.bfloat16)
+    sub = lax.broadcasted_iota(jnp.int32, (16, LANES), 0)
+
+    def keep_ids():
+        table = jnp.full((16, LANES), -1.0, jnp.float32)
+        for r in range(owners):
+            table = jnp.where(sub == r, locals_in[r].astype(jnp.float32), table)
+        id_tile[...] = table.astype(jnp.bfloat16)
 
     def collect_ids():
         small = [None]
@@ -124,9 +127,8 @@
         for r in range(1, owners):
             small[r].wait()
             locals_in.append(id_smem[r, 0, 0])
-            keep_id(r)
-
-    keep_id(0)
+        keep_ids()
+
     def hops(direction, block):
         longer = replicas // 2
         first = block < owners // 2
@@ -159,8 +161,9 @@
 
     def add_gram(parts):
         kept = []
-        for rows, ids in parts:
-            match = (ids.astype(jnp.float32) == mine.astype(jnp.float32)).astype(jnp.float32)
+        for rows, table, b in parts:
+            ids = table.astype(jnp.float32)[b : b + 1, :]
+            match = (ids == mine.astype(jnp.float32)).astype(jnp.float32)
             match = jnp.concatenate([match] * (width // LANES), axis=1)
             kept.append((rows.astype(jnp.float32) * match).astype(jnp.bfloat16))
         kept = jnp.concatenate(kept, axis=0)
@@ -207,7 +210,7 @@
                 collect_ids()
                 for d in range(2):
                     send_ids(d, 1)
-            add_gram([(hidden[b], id_tile[b * 16 : b * 16 + 1, :])])
+            add_gram([(hidden[b], id_tile[...], b)])
         else:
             parts = []
             for d in range(2):
@@ -220,7 +223,7 @@
                 moves[d, hop, b].wait_recv()
                 send_block(d, hop + 1, b)
                 parts.append((d, hop - 1))
-            add_gram([(ring[d, h, b], id_ring[d, h, b * 16 : b * 16 + 1, :]) for d, h in parts])
+            add_gram([(ring[d, h, b], id_ring[d, h], b) for d, h in parts])
     for copy in sent:
         copy.wait_send()
     row = lax.broadcasted_iota(jnp.int32, (width, width), 0)
@@ -252,8 +255,8 @@
             pltpu.VMEM((owners, 8, LANES), jnp.int32),
             pltpu.VMEM((owners, 8, LANES), jnp.int32),
             pltpu.SMEM((owners, 8, LANES), jnp.int32),
-            pltpu.VMEM((owners * 16, LANES), bf16),
-            pltpu.VMEM((2, longest, owners * 16, LANES), bf16),
+            pltpu.VMEM((16, LANES), bf16),
+            pltpu.VMEM((2, longest, 16, LANES), bf16),
             pltpu.VMEM((owners, BLOCK, width), bf16),
             pltpu.VMEM((2, longest, owners, BLOCK, width), bf16),
             dma((3,)),
@@ -264,7 +267,7 @@
             dma((2, longest, 2)),
         ],
         compiler_params=pltpu.CompilerParams(
-            collective_id=0, has_side_effects=True, vmem_limit_bytes=52 * 1024 * 1024
+            collective_id=0, has_side_effects=True, vmem_limit_bytes=60 * 1024 * 1024
         ),
         name="grams",
     )(block_expert, tokens.reshape(-1, BLOCK, model), gate_weight, up_weight)

time: 70.6 us -> 70 us (level)
  local copies, waits for them, and re-layouts: 2.7 us -> 1.87 us
    pallas_call x1, Pallas kernels: 45 us -> 46.9 us  [grams(): pl.pallas_call(functools.partial(gram_kernel, owners, replicas, experts,...]
    pallas_call x1, Pallas kernels: 22.7 us -> 21.1 us  [factored_rows(): pl.pallas_call(functools.partial(factor_kernel, replicas, replicas // exp...]
    unnamed x5 -> x3, local copies, waits for them, and re-layouts: 2.7 us -> 1.87 us
where the time goes in v5:
time: 70 us; the launch traced here: 69.8 us
  Pallas kernels  67.9 us (97%)
  local copies, waits for them, and re-layouts  1.87 us (3%)
    pallas_call x1, Pallas kernels, grams(): pl.pallas_call(functools.partial(gram_kernel, owners, replicas, experts,...  46.9 us
    pallas_call x1, Pallas kernels, factored_rows(): pl.pallas_call(functools.partial(factor_kernel, replicas, replicas // exp...  21.1 us
    unnamed x3, local copies, waits for them, and re-layouts  1.87 us

profile of v5, /device:TPU:0, one launch (start us, length us, event | category | flops | bytes accessed | tf_op | source)
XLA Modules:
  0.0 69.8 jit_solution(1730612769526594385)
XLA Ops:
  0.0 46.9 %grams.1.gram_ref = f32[384,384]{1,0:T(8,128)} custom-call(s32[4]{0:T(128)} %expert_ref.1, bf16[4,128,1024]{2,1,0:T(8,128)(2,1)} %bitcast.1, bf16[8,1024,384]{2,1,0:T(8,128)(2,1)} %gate_hbm.1, bf16[8,1024,384]{2,1,0:T(8,128)(2,1)} %up_hbm.1), custom_call_target="tpu_custom_call" | custom-call | tf_op jit(solution)/shard_map/grams/pallas_call | solution.py:244
  46.9 0.0 copy-start
  46.9 1.1 %copy-done = f32[384,384]{1,0:T(8,128)S(1)} copy-done((f32[384,384]{1,0:T(8,128)S(1)}, f32[384,384]{1,0:T(8,128)}, u32[]{:S(2)}) %copy-start) | copy-done | bytes 589848
  47.9 21.1 %factored_rows.1 = f32[8,48,384]{2,1,0:T(8,128)S(1)} custom-call(f32[384,384]{1,0:T(8,128)S(1)} %copy-done), custom_call_target="tpu_custom_call" | custom-call | tf_op jit(solution)/shard_map/factored_rows/pallas_call | solution.py:429
  69.0 0.8 %copy.6 = f32[8,48,384]{2,1,0:T(8,128)} copy(f32[8,48,384]{2,1,0:T(8,128)S(1)} %factored_rows.1) | data formatting | bytes 1179648
Async XLA Ops:
  46.9 1.1 %copy-start = (f32[384,384]{1,0:T(8,128)S(1)}, f32[384,384]{1,0:T(8,128)}, u32[]{:S(2)}) copy-start(f32[384,384]{1,0:T(8,128)} %grams.1.gram_ref) | copy-start | bytes 1769476
